TPU v7x, 32 devices: a whole 2x2x4 slice. The times are simulated.
32 devices in a mesh: dp: 16 (over z, x, core), fsdp: 2 (over y).
Axes of the slice: x: 2, y: 2, z: 4, core: 2. Of those that a mesh axis runs over, the one named last changes fastest.
Arguments:
- tokens: bfloat16 [4, 16384, 768], P(None, ('dp', 'fsdp')), may hold values from -6 to 6
- lengths: int32 [4, 32, 8], P(None, ('dp', 'fsdp')), may hold values from 0 to 512, as said below
- cotangent: bfloat16 [4, 16384, 768], P(None, ('dp', 'fsdp')), may hold values from -6 to 6
- attn_norm_gain: bfloat16 [768], P(('dp', 'fsdp')), may hold values from 0.5 to 1.5
- attn_norm_bias: bfloat16 [768], P(('dp', 'fsdp')), may hold values from -1 to 1
- qkv_weight: bfloat16 [768, 2304], P(('dp', 'fsdp')), may hold values from -0.21875 to 0.21875
- qkv_bias: bfloat16 [2304], P(('dp', 'fsdp')), may hold values from -1 to 1
- out_weight: bfloat16 [768, 768], P(('dp', 'fsdp')), may hold values from -0.625 to 0.625
- out_bias: bfloat16 [768], P(('dp', 'fsdp')), may hold values from -1 to 1
- mlp_norm_gain: bfloat16 [768], P(('dp', 'fsdp')), may hold values from 0.5 to 1.5
- mlp_norm_bias: bfloat16 [768], P(('dp', 'fsdp')), may hold values from -1 to 1
- up_weight: bfloat16 [768, 3072], P(('dp', 'fsdp')), may hold values from -0.21875 to 0.21875
- up_bias: bfloat16 [3072], P(('dp', 'fsdp')), may hold values from -1 to 1
- down_weight: bfloat16 [3072, 768], P(('dp', 'fsdp')), may hold values from -0.109375 to 0.109375
- down_bias: bfloat16 [768], P(('dp', 'fsdp')), may hold values from -1 to 1
Outputs:
- block_out: bfloat16 [4, 16384, 768], P(None, ('dp', 'fsdp'))
- grad_tokens: bfloat16 [4, 16384, 768], P(None, ('dp', 'fsdp'))
- grad_attn_norm_gain: float32 [768], P(('dp', 'fsdp'))
- grad_attn_norm_bias: float32 [768], P(('dp', 'fsdp'))
- grad_qkv_weight: float32 [768, 2304], P(('dp', 'fsdp'))
- grad_qkv_bias: float32 [2304], P(('dp', 'fsdp'))
- grad_out_weight: float32 [768, 768], P(('dp', 'fsdp'))
- grad_out_bias: float32 [768], P(('dp', 'fsdp'))
- grad_mlp_norm_gain: float32 [768], P(('dp', 'fsdp'))
- grad_mlp_norm_bias: float32 [768], P(('dp', 'fsdp'))
- grad_up_weight: float32 [768, 3072], P(('dp', 'fsdp'))
- grad_up_bias: float32 [3072], P(('dp', 'fsdp'))
- grad_down_weight: float32 [3072, 768], P(('dp', 'fsdp'))
- grad_down_bias: float32 [768], P(('dp', 'fsdp'))
Inputs may be any that keep to these rules, and one draw needn't show every extreme that they name: Each row lists the lengths of the sequences packed into one row of 512 positions, in order: a slot holds 0 (unused, only after all used ones) or 64 to 512; a row's lengths sum to at most 512; in every draw some row holds one sequence of 512.
All inputs are finite; a program needn't handle non-finite values.
Results may differ from a plain program's by a relative error of at most 0.01.
Values may be sent and summed in bfloat16 or wider, within the bound.
No kernel may reach another device: no remote copies, remote signals or barrier semaphores. Data moves between devices by JAX's collectives and lax.ppermute only.
A program may use at most 320 MiB of HBM per device.

v0:
```python
import jax
import jax.numpy as jnp
from jax import lax
from jax.sharding import PartitionSpec as P

HEADS = 12
HEAD = 64


def layer_norm(inputs, gain, shift):
    centred = inputs - jnp.mean(inputs, axis=-1, keepdims=True)
    spread = jnp.mean(centred * centred, axis=-1, keepdims=True)
    return centred * lax.rsqrt(spread + 1e-05) * gain + shift


def seq_masks(seq_lens, row_count):
    seq_ends = jnp.cumsum(seq_lens, dtype=jnp.int32)
    places = jnp.arange(row_count, dtype=jnp.int32)
    segment = jnp.sum((seq_ends[None, :] <= places[:, None]).astype(jnp.int32), axis=1)
    allowed = (segment[:, None] == segment[None, :]) & (places[None, :] <= places[:, None])
    valid = (places < seq_ends[-1]).astype(jnp.float32)
    return (valid, allowed)


def cross_rows(left, right):
    return lax.dot_general(
        left, right, (((0,), (0,)), ((), ())), preferred_element_type=jnp.float32
    )


def back_mult(grad_rows, weight):
    return lax.dot_general(
        grad_rows, weight, (((1,), (1,)), ((), ())), preferred_element_type=jnp.float32
    )


def split_heads(merged):
    row_count = merged.shape[0]
    width = merged.shape[1] // 3
    return tuple(
        (
            merged[:, section * width : (section + 1) * width].reshape(row_count, HEADS, HEAD)
            for section in range(3)
        )
    )


def head_scores(queries, keys_all):
    return jnp.einsum(
        "qhd,khd->hqk", queries, keys_all, preferred_element_type=jnp.float32
    ) * HEAD ** (-0.5)


def score_total(scores, allowed):
    magnitude = jnp.sqrt(scores * scores + 1.0)
    masked = jnp.where(allowed[None], magnitude, -jnp.inf)
    row_top = jnp.max(masked, axis=-1, keepdims=True)
    return row_top + jnp.log(jnp.sum(jnp.exp(masked - row_top), axis=-1, keepdims=True))


def signed_parts(scores, allowed, log_total):
    magnitude = jnp.sqrt(scores * scores + 1.0)
    exp_part = jnp.exp(jnp.where(allowed[None], magnitude - log_total, -jnp.inf))
    smooth_sign = jnp.tanh(scores)
    return (magnitude, exp_part, smooth_sign, smooth_sign * exp_part)


def as_floats(params):
    return tuple((item.astype(jnp.float32) if item.ndim == 1 else item for item in params))


def forward_row(params, inputs, seq_lens):
    (
        gain_one,
        bias_one,
        weight_qkv,
        bias_qkv,
        weight_out,
        bias_out,
        gain_two,
        bias_two,
        weight_up,
        bias_up,
        weight_down,
        bias_down,
    ) = as_floats(params)
    row_count = inputs.shape[0]
    valid, allowed = seq_masks(seq_lens, row_count)
    residual = inputs.astype(jnp.float32)
    normed_one = layer_norm(residual, gain_one, bias_one).astype(jnp.bfloat16)
    merged = (
        jnp.dot(normed_one, weight_qkv, preferred_element_type=jnp.float32) + bias_qkv
    ).astype(jnp.bfloat16)
    queries, keys_all, values_all = split_heads(merged)
    scores = head_scores(queries, keys_all)
    log_total = score_total(scores, allowed)
    signed = signed_parts(scores, allowed, log_total)[3]
    mixed = jnp.einsum(
        "hqk,khd->qhd", signed.astype(jnp.bfloat16), values_all, preferred_element_type=jnp.float32
    )
    mixed = mixed.reshape(row_count, -1).astype(jnp.bfloat16)
    hidden = residual + jnp.dot(mixed, weight_out, preferred_element_type=jnp.float32) + bias_out
    normed_two = layer_norm(hidden, gain_two, bias_two).astype(jnp.bfloat16)
    pre_act = jnp.dot(normed_two, weight_up, preferred_element_type=jnp.float32) + bias_up
    activated = jax.nn.gelu(pre_act).astype(jnp.bfloat16)
    result = (
        hidden + jnp.dot(activated, weight_down, preferred_element_type=jnp.float32) + bias_down
    )
    saved_state = (
        residual,
        normed_one,
        merged,
        log_total,
        mixed,
        hidden,
        normed_two,
        pre_act,
        activated,
        valid,
        allowed,
    )
    return (saved_state, result.astype(jnp.bfloat16))


def backward_row(params, saved_state, cotangent):
    (
        gain_one,
        bias_one,
        weight_qkv,
        bias_qkv,
        weight_out,
        bias_out,
        gain_two,
        bias_two,
        weight_up,
        bias_up,
        weight_down,
        bias_down,
    ) = as_floats(params)
    (
        residual,
        normed_one,
        merged,
        log_total,
        mixed,
        hidden,
        normed_two,
        pre_act,
        activated,
        valid,
        allowed,
    ) = saved_state
    row_count = residual.shape[0]
    out_grad = cotangent.astype(jnp.float32) * valid[:, None]
    down_grad = out_grad.astype(jnp.bfloat16)
    grad_down = cross_rows(activated, down_grad)
    grad_bias_down = jnp.sum(down_grad.astype(jnp.float32), axis=0)
    act_grad = back_mult(down_grad, weight_down)
    gelu_back = jax.vjp(jax.nn.gelu, pre_act)[1]
    up_grad = gelu_back(act_grad)[0].astype(jnp.bfloat16)
    grad_up = cross_rows(normed_two, up_grad)
    grad_bias_up = jnp.sum(up_grad.astype(jnp.float32), axis=0)
    normed_grad = back_mult(up_grad, weight_up)
    second_back = jax.vjp(layer_norm, hidden, gain_two, bias_two)[1]
    hidden_part, grad_gain_two, grad_bias_two = second_back(normed_grad)
    hidden_grad = out_grad + hidden_part
    proj_grad = hidden_grad.astype(jnp.bfloat16)
    grad_out = cross_rows(mixed, proj_grad)
    grad_bias_out = jnp.sum(proj_grad.astype(jnp.float32), axis=0)
    mixed_grad = (
        back_mult(proj_grad, weight_out).astype(jnp.bfloat16).reshape(row_count, HEADS, HEAD)
    )
    queries, keys_all, values_all = split_heads(merged)
    scores = head_scores(queries, keys_all)
    magnitude, exp_part, smooth_sign, signed = signed_parts(scores, allowed, log_total)
    weight_grad = jnp.einsum(
        "qhd,khd->hqk", mixed_grad, values_all, preferred_element_type=jnp.float32
    )
    centre = jnp.sum(weight_grad * signed, axis=-1, keepdims=True)
    score_grad = exp_part * (
        weight_grad * (1.0 - smooth_sign * smooth_sign)
        + scores / magnitude * (weight_grad * smooth_sign - centre)
    )
    score_grad = score_grad.astype(jnp.bfloat16)
    query_grad = jnp.einsum(
        "hqk,khd->qhd", score_grad, keys_all, preferred_element_type=jnp.float32
    ) * HEAD ** (-0.5)
    key_grad = jnp.einsum(
        "hqk,qhd->khd", score_grad, queries, preferred_element_type=jnp.float32
    ) * HEAD ** (-0.5)
    value_grad = jnp.einsum(
        "hqk,qhd->khd", signed.astype(jnp.bfloat16), mixed_grad, preferred_element_type=jnp.float32
    )
    merged_grad = jnp.concatenate(
        [
            query_grad.reshape(row_count, -1),
            key_grad.reshape(row_count, -1),
            value_grad.reshape(row_count, -1),
        ],
        axis=1,
    ).astype(jnp.bfloat16)
    grad_qkv = cross_rows(normed_one, merged_grad)
    grad_bias_qkv = jnp.sum(merged_grad.astype(jnp.float32), axis=0)
    first_grad = back_mult(merged_grad, weight_qkv)
    first_back = jax.vjp(layer_norm, residual, gain_one, bias_one)[1]
    resid_part, grad_gain_one, grad_bias_one = first_back(first_grad)
    input_grad = (hidden_grad + resid_part).astype(jnp.bfloat16)
    gradients = (
        grad_gain_one,
        grad_bias_one,
        grad_qkv,
        grad_bias_qkv,
        grad_out,
        grad_bias_out,
        grad_gain_two,
        grad_bias_two,
        grad_up,
        grad_bias_up,
        grad_down,
        grad_bias_down,
    )
    return (gradients, input_grad)


def on_device(
    tokens,
    lengths,
    cotangent,
    attn_norm_gain,
    attn_norm_bias,
    qkv_weight,
    qkv_bias,
    out_weight,
    out_bias,
    mlp_norm_gain,
    mlp_norm_bias,
    up_weight,
    up_bias,
    down_weight,
    down_bias,
):
    shards = (
        attn_norm_gain,
        attn_norm_bias,
        qkv_weight,
        qkv_bias,
        out_weight,
        out_bias,
        mlp_norm_gain,
        mlp_norm_bias,
        up_weight,
        up_bias,
        down_weight,
        down_bias,
    )
    micro_count = tokens.shape[0]
    outputs = []
    input_grads = []
    totals = None
    collected = None
    for batch_step in range(micro_count):
        params = (
            lax.all_gather(shards[0], ("dp", "fsdp"), axis=0, tiled=True),
            lax.all_gather(shards[1], ("dp", "fsdp"), axis=0, tiled=True),
            lax.all_gather(shards[2], ("dp", "fsdp"), axis=0, tiled=True),
            lax.all_gather(shards[3], ("dp", "fsdp"), axis=0, tiled=True),
            lax.all_gather(shards[4], ("dp", "fsdp"), axis=0, tiled=True),
            lax.all_gather(shards[5], ("dp", "fsdp"), axis=0, tiled=True),
            lax.all_gather(shards[6], ("dp", "fsdp"), axis=0, tiled=True),
            lax.all_gather(shards[7], ("dp", "fsdp"), axis=0, tiled=True),
            lax.all_gather(shards[8], ("dp", "fsdp"), axis=0, tiled=True),
            lax.all_gather(shards[9], ("dp", "fsdp"), axis=0, tiled=True),
            lax.all_gather(shards[10], ("dp", "fsdp"), axis=0, tiled=True),
            lax.all_gather(shards[11], ("dp", "fsdp"), axis=0, tiled=True),
        )
        saved_state, result = forward_row(params, tokens[batch_step], lengths[batch_step, 0])
        outputs.append(result)
        params_back = (
            lax.all_gather(shards[0], ("dp", "fsdp"), axis=0, tiled=True),
            lax.all_gather(shards[1], ("dp", "fsdp"), axis=0, tiled=True),
            lax.all_gather(shards[2], ("dp", "fsdp"), axis=0, tiled=True),
            lax.all_gather(shards[3], ("dp", "fsdp"), axis=0, tiled=True),
            lax.all_gather(shards[4], ("dp", "fsdp"), axis=0, tiled=True),
            lax.all_gather(shards[5], ("dp", "fsdp"), axis=0, tiled=True),
            lax.all_gather(shards[6], ("dp", "fsdp"), axis=0, tiled=True),
            lax.all_gather(shards[7], ("dp", "fsdp"), axis=0, tiled=True),
            lax.all_gather(shards[8], ("dp", "fsdp"), axis=0, tiled=True),
            lax.all_gather(shards[9], ("dp", "fsdp"), axis=0, tiled=True),
            lax.all_gather(shards[10], ("dp", "fsdp"), axis=0, tiled=True),
            lax.all_gather(shards[11], ("dp", "fsdp"), axis=0, tiled=True),
        )
        gradients, input_grad = backward_row(params_back, saved_state, cotangent[batch_step])
        input_grads.append(input_grad)
        if batch_step == 0:
            totals = gradients
        else:
            totals = tuple((first + second for first, second in zip(totals, gradients)))
    collected = lax.psum_scatter(totals, ("dp", "fsdp"), scatter_dimension=0, tiled=True)
    return (jnp.stack(outputs, axis=0), jnp.stack(input_grads, axis=0)) + tuple(collected)


def solution(mesh):
    placed = (
        P(None, ("dp", "fsdp"), None),
        P(None, ("dp", "fsdp"), None),
        P(None, ("dp", "fsdp"), None),
        P(("dp", "fsdp")),
        P(("dp", "fsdp")),
        P(("dp", "fsdp"), None),
        P(("dp", "fsdp")),
        P(("dp", "fsdp"), None),
        P(("dp", "fsdp")),
        P(("dp", "fsdp")),
        P(("dp", "fsdp")),
        P(("dp", "fsdp"), None),
        P(("dp", "fsdp")),
        P(("dp", "fsdp"), None),
        P(("dp", "fsdp")),
    )
    return jax.shard_map(
        on_device,
        mesh=mesh,
        in_specs=placed,
        out_specs=(
            P(None, ("dp", "fsdp"), None),
            P(None, ("dp", "fsdp"), None),
            P(("dp", "fsdp")),
            P(("dp", "fsdp")),
            P(("dp", "fsdp"), None),
            P(("dp", "fsdp")),
            P(("dp", "fsdp"), None),
            P(("dp", "fsdp")),
            P(("dp", "fsdp")),
            P(("dp", "fsdp")),
            P(("dp", "fsdp"), None),
            P(("dp", "fsdp")),
            P(("dp", "fsdp"), None),
            P(("dp", "fsdp")),
        ),
        check_vma=False,
    )
```

profile of v0, /device:TPU:0, one launch (start us, length us, event | category | flops | bytes accessed | tf_op | source)
XLA Modules:
  0.0 1088.1 jit_solution(16744467387025519731)
XLA Ops:
  16.8 42.7 %all-reduce.17 = (bf16[2304]{0:T(1024)(128)(2,1)S(1)}, bf16[768]{0:T(1024)(128)(2,1)S(1)}, bf16[768]{0:T(1024)(128)(2,1)S(1)}, bf16[768]{0:T(1024)(128)(2,1)S(1)...) all-reduce(bf16[2304]{0:T(1024)(128)(2,1)S(1)} %dynamic-update-slic, ...), channel_id=1, replica_groups=mesh['dp'=16,'fsdp'=2] {'dp','fsdp'}, use_global_device_ids=true, to_apply=%add.2 | all-reduce | flops 9984 | bytes 39936
  86.5 9.0 fusion.15
  102.3 8.9 fusion.154
  111.3 18.5 %all-gather.7.cloned.1.call-done = bf16[768,768]{1,0:T(8,128)(2,1)} async-done(((bf16[24,768]{1,0:T(8,128)(2,1)}), bf16[768,768]{1,0:T(8,128)(2,1)}) %all-gather.7.cloned.1.call-update) | async-done | bytes 1179664 | tf_op jit(solution)/shard_map/all_gather | solution.py:267
  172.5 11.6 %fusion.148 = bf16[12,64,512]{2,1,0:T(8,128)(2,1)S(1)} fusion(bf16[512,12,64]{0,2,1:T(8,128)(2,1)} %bitcast.457, f32[12,512,512]{1,2,0:T(8,128)} %copy-done.22, f32[12,512]{1,0:T(8,128)S(1)} %log_add_fusion.1, pred[512,512]{0,1:T(8,128)(4,1)} %fusion.173), kind=kOutput, calls=%fused_computation.254 | convolution fusion | flops 425066496 | bytes 14442496 | tf_op jit(solution)/shard_map/hqk,khd->qhd/dot_general | solution.py:98
  199.9 8.4 fusion.142
  210.5 8.4 fusion.244
  228.5 32.1 %all-gather.11.cloned.1.call-done = bf16[3072,768]{1,0:T(8,128)(2,1)} async-done(((bf16[96,768]{1,0:T(8,128)(2,1)}), bf16[3072,768]{1,0:T(8,128)(2,1)}) %all-gather.11.cloned.1.call-update) | async-done | bytes 4718608 | tf_op jit(solution)/shard_map/all_gather | solution.py:273
  260.6 9.7 convert_reduce_fusion
  277.1 8.7 convert_reduce_fusion.2
  288.6 8.5 convert_reduce_fusion.1
  307.7 12.6 %fusion.157 = bf16[12,64,512]{2,1,0:T(8,128)(2,1)} fusion(bf16[512,12,64]{0,2,1:T(8,128)(2,1)S(1)} %bitcast.463, f32[12,512,512]{1,2,0:T(8,128)} %copy-done.21, f32[12,512]{1,0:T(8,128)S(1)} %log_add_fusion, pred[512,512]{0,1:T(8,128)(4,1)S(1)} %copy-done.89), kind=kOutput, calls=%fused_computation.257 | convolution fusion | flops 425066496 | bytes 14442496 | tf_op jit(solution)/shard_map/hqk,qhd->khd/dot_general | solution.py:191
  320.3 26.5 %multiply_convert_fusion = bf16[12,512,512]{1,2,0:T(8,128)(2,1)} fusion(f32[12,512,512]{1,2,0:T(8,128)} %copy-done.21, f32[12,512]{1,0:T(8,128)S(1)} %log_add_fusion, pred[512,512]{0,1:T(8,128)(4,1)S(1)} %copy-done.89, bf16[512,12,64]{0,2,1:T(8,128)(2,1)S(1)} %bitcast.464, bf16[512,12,64]{0,2,1:T(8,128)(2,1)S(1)} %bitcast.454), kind=kOutput, calls=%fused_computation.4 | convolution fusion | flops 874519040 | bytes 20733952 | tf_op jit(solution)/shard_map/sub | solution.py:182
  355.9 12.5 %fusion.151 = bf16[12,64,512]{2,1,0:T(8,128)(2,1)} fusion(bf16[512,12,64]{0,2,1:T(8,128)(2,1)S(1)} %bitcast.465, f32[12,512,512]{1,2,0:T(8,128)} %copy-done.22, f32[12,512]{1,0:T(8,128)S(1)} %copy-done.122, pred[512,512]{0,1:T(8,128)(4,1)S(1)} %copy-done.87), kind=kOutput, calls=%fused_computation.255 | convolution fusion | flops 425066496 | bytes 14442496 | tf_op jit(solution)/shard_map/hqk,qhd->khd/dot_general | solution.py:191
  368.4 26.3 %multiply_convert_fusion.1 = bf16[12,512,512]{1,2,0:T(8,128)(2,1)} fusion(f32[12,512,512]{1,2,0:T(8,128)} %copy-done.22, f32[12,512]{1,0:T(8,128)S(1)} %copy-done.122, pred[512,512]{0,1:T(8,128)(4,1)S(1)} %copy-done.87, bf16[512,12,64]{0,2,1:T(8,128)(2,1)S(1)} %bitcast.466, bf16[512,12,64]{0,2,1:T(8,128)(2,1)S(1)} %bitcast.458), kind=kOutput, calls=%fused_computation.8 | convolution fusion | flops 874519040 | bytes 20733952 | tf_op jit(solution)/shard_map/sub | solution.py:182
  403.8 12.9 %fusion.145 = bf16[12,64,512]{2,1,0:T(8,128)(2,1)} fusion(bf16[512,12,64]{0,2,1:T(8,128)(2,1)S(1)} %bitcast.467, f32[12,512,512]{1,2,0:T(8,128)} %copy-done.23, f32[12,512]{1,0:T(8,128)S(1)} %copy-done.124, pred[512,512]{0,1:T(8,128)(4,1)S(1)} %copy-done.85), kind=kOutput, calls=%fused_computation.253 | convolution fusion | flops 425066496 | bytes 14442496 | tf_op jit(solution)/shard_map/hqk,qhd->khd/dot_general | solution.py:191
  416.6 26.3 %multiply_convert_fusion.2 = bf16[12,512,512]{1,2,0:T(8,128)(2,1)} fusion(f32[12,512,512]{1,2,0:T(8,128)} %copy-done.23, f32[12,512]{1,0:T(8,128)S(1)} %copy-done.124, pred[512,512]{0,1:T(8,128)(4,1)S(1)} %copy-done.85, bf16[512,12,64]{0,2,1:T(8,128)(2,1)S(1)} %bitcast.468, bf16[512,12,64]{0,2,1:T(8,128)(2,1)S(1)} %bitcast.456), kind=kOutput, calls=%fused_computation.12 | convolution fusion | flops 874519040 | bytes 20733952 | tf_op jit(solution)/shard_map/sub | solution.py:182
  484.6 8.8 fusion.12
  500.1 8.6 fusion.136
  512.9 9.1 convert_reduce_fusion.3
  535.5 28.9 %multiply_convert_fusion.3 = bf16[12,512,512]{1,2,0:T(8,128)(2,1)} fusion(f32[12,512,512]{1,2,0:T(8,128)} %copy-done.24, f32[12,512]{1,0:T(8,128)S(1)} %log_add_fusion.3, pred[512,512]{0,1:T(8,128)(4,1)S(1)} %copy-done.83, bf16[512,12,64]{0,2,1:T(8,128)(2,1)} %bitcast.461, bf16[512,12,64]{0,2,1:T(8,128)(2,1)} %bitcast.459), kind=kOutput, calls=%fused_computation.16 | convolution fusion | flops 874519040 | bytes 20733952 | tf_op jit(solution)/shard_map/sub | solution.py:182
  578.3 11.9 %fusion.139 = bf16[12,64,512]{2,1,0:T(8,128)(2,1)S(1)} fusion(bf16[512,12,64]{0,2,1:T(8,128)(2,1)S(1)} %bitcast.462, f32[12,512,512]{1,2,0:T(8,128)} %copy-done.24, f32[12,512]{1,0:T(8,128)S(1)} %log_add_fusion.3, pred[512,512]{0,1:T(8,128)(4,1)S(1)} %copy-done.83), kind=kOutput, calls=%fused_computation.251 | convolution fusion | flops 425066496 | bytes 14442496 | tf_op jit(solution)/shard_map/hqk,qhd->khd/dot_general | solution.py:191
  595.5 10.7 add_add_fusion.2
  606.9 9.1 fusion.242
  627.3 16.5 %add_add_fusion.1 = f32[768,3072]{1,0:T(8,128)} fusion(f32[768,3072]{1,0:T(8,128)} %fusion.242, f32[768,3072]{1,0:T(8,128)} %fusion.238, f32[768,3072]{1,0:T(8,128)} %fusion.240, bf16[512,3072]{1,0:T(8,128)(2,1)S(1)} %copy-done.58, f32[512,768]{1,0:T(8,128)S(1)} %copy-done.12, f32[512]{0:T(512)S(1)} %copy-done.137, f32[512]{0:T(512)S(1)} %copy-done.120, ...), kind=kOutput, calls=%fused_computation.37 | convolution fusion | flops 2424963072 | bytes 42477568 | tf_op jit(solution)/shard_map/dot_general | solution.py:26
  644.5 10.4 fusion.208
  654.9 10.2 fusion.196
  671.6 18.8 %add_add_fusion = f32[3072,768]{1,0:T(8,128)} fusion(f32[3072,768]{1,0:T(8,128)} %fusion.208, f32[3072,768]{1,0:T(8,128)} %fusion.196, f32[3072,768]{1,0:T(8,128)} %fusion.202, f32[512]{0:T(512)S(1)} %copy-done.111, bf16[4,512,768]{2,1,0:T(8,128)(2,1)S(1)} %copy-done.7, f32[512,3072]{1,0:T(8,128)} %fusion.244, f32[3072]{0:T(1024)S(1)} %copy-done.113), kind=kOutput, calls=%fused_computation.36 | convolution fusion | flops 2439905280 | bytes 44840960 | tf_op jit(solution)/shard_map/dot_general | solution.py:26
  707.1 41.9 %all-reduce.16 = (f32[768]{0:T(1024)S(1)}, f32[768]{0:T(1024)S(1)}, f32[2304]{0:T(1024)S(1)}, f32[768]{0:T(1024)S(1)}, f32[768]{0:T(1024)S(1)}, /*index=5*/f32[7...) all-reduce(f32[768]{0:T(1024)S(1)} %add_add_fusion.19, ...), channel_id=2, replica_groups=mesh['dp'=16,'fsdp'=2] {'dp','fsdp'}, use_global_device_ids=true, to_apply=%region_56.57.clone | all-reduce | flops 9984 | bytes 79872
  753.7 8.8 fusion.171
  797.5 141.3 %reduce-scatter.9.cloned.1.call-done = f32[24,3072]{1,0:T(8,128)} async-done(((f32[768,3072]{1,0:T(8,128)}), f32[24,3072]{1,0:T(8,128)}) %reduce-scatter.9.cloned.1.call-update) | async-done | bytes 294928 | tf_op jit(solution)/shard_map/reduce_scatter | solution.py:298
  938.8 142.3 %reduce-scatter.11.cloned.1.call-done = f32[96,768]{1,0:T(8,128)} async-done(((f32[3072,768]{1,0:T(8,128)}), f32[96,768]{1,0:T(8,128)}) %reduce-scatter.11.cloned.1.call-update) | async-done | bytes 294928 | tf_op jit(solution)/shard_map/reduce_scatter | solution.py:298
  (673 shorter events, 309.7 us)
Async XLA Ops:
  7.2 55.3 %copy-start.3 = (bf16[4,512,768]{2,1,0:T(8,128)(2,1)S(1)}, bf16[4,512,768]{2,1,0:T(8,128)(2,1)}, u32[]{:S(2)}) copy-start(bf16[4,512,768]{2,1,0:T(8,128)(2,1)} %param.15) | copy-start | bytes 9437188
  7.2 56.2 %copy-start.198 = (s32[4,1,8]{2,1,0:T(1,128)S(1)}, s32[4,1,8]{2,1,0:T(1,128)}, u32[]{:S(2)}) copy-start(s32[4,1,8]{2,1,0:T(1,128)} %param.16) | copy-start | bytes 388
  7.2 66.7 %all-gather.5.cloned.1.call-start = ((), (), s32[]{:S(2)}) async-start(), calls=%async_computation.4 | async-start | bytes 3649536 | tf_op jit(solution)/shard_map/all_gather | solution.py:265
  7.9 121.9 %all-gather.7.cloned.1.call-start = ((), (), s32[]{:S(2)}) async-start(), calls=%async_computation.5 | async-start | bytes 1216512 | tf_op jit(solution)/shard_map/all_gather | solution.py:267
  8.7 201.8 %all-gather.9.cloned.1.call-start = ((), (), s32[]{:S(2)}) async-start(), calls=%async_computation.6 | async-start | bytes 4866048 | tf_op jit(solution)/shard_map/all_gather | solution.py:271
  9.4 251.2 %all-gather.11.cloned.1.call-start = ((), (), s32[]{:S(2)}) async-start(), calls=%async_computation.7 | async-start | bytes 4866048 | tf_op jit(solution)/shard_map/all_gather | solution.py:273
  10.0 780.0 %reduce-scatter.7.cloned.1.call-start = ((), (), s32[]{:S(2)}) async-start(), calls=%async_computation.9 | async-start | bytes 2433024 | tf_op jit(solution)/shard_map/reduce_scatter | solution.py:298
  59.5 148.9 %copy-start.192 = (f32[768]{0:T(1024)}, f32[768]{0:T(1024)S(1)}, u32[]{:S(2)}) copy-start(f32[768]{0:T(1024)S(1)} %convert_element_type.392) | copy-start | bytes 9220
  59.5 82.3 %copy-start.167 = (f32[2304]{0:T(1024)}, f32[2304]{0:T(1024)S(1)}, u32[]{:S(2)}) copy-start(f32[2304]{0:T(1024)S(1)} %convert_element_type.385) | copy-start | bytes 27652
  62.5 79.3 %copy-start.140 = (f32[512]{0:T(512)}, f32[512]{0:T(512)S(1)}, u32[]{:S(2)}) copy-start(f32[512]{0:T(512)S(1)} %get-tuple-element.151) | copy-start | bytes 6148
  62.5 71.0 %copy-start.114 = (f32[512]{0:T(512)}, f32[512]{0:T(512)S(1)}, u32[]{:S(2)}) copy-start(f32[512]{0:T(512)S(1)} %get-tuple-element.150) | copy-start | bytes 6148
  63.4 78.4 %copy-start.165 = (f32[768]{0:T(1024)}, f32[768]{0:T(1024)S(1)}, u32[]{:S(2)}) copy-start(f32[768]{0:T(1024)S(1)} %convert_element_type.383) | copy-start | bytes 9220
  63.4 78.4 %copy-start.106 = (f32[768]{0:T(1024)}, f32[768]{0:T(1024)S(1)}, u32[]{:S(2)}) copy-start(f32[768]{0:T(1024)S(1)} %convert_element_type.382) | copy-start | bytes 9220
  65.2 158.5 %copy-start.163 = (f32[768]{0:T(1024)}, f32[768]{0:T(1024)S(1)}, u32[]{:S(2)}) copy-start(f32[768]{0:T(1024)S(1)} %convert_element_type.394) | copy-start | bytes 9220
  65.2 235.8 %copy-start.108 = (f32[768]{0:T(1024)}, f32[768]{0:T(1024)S(1)}, u32[]{:S(2)}) copy-start(f32[768]{0:T(1024)S(1)} %convert_element_type.393) | copy-start | bytes 9220
  65.2 223.3 %copy-start.112 = (f32[3072]{0:T(1024)}, f32[3072]{0:T(1024)S(1)}, u32[]{:S(2)}) copy-start(f32[3072]{0:T(1024)S(1)} %convert_element_type.396) | copy-start | bytes 36868
  65.2 68.2 %copy-start.131 = (f32[512]{0:T(512)}, f32[512]{0:T(512)S(1)}, u32[]{:S(2)}) copy-start(f32[512]{0:T(512)S(1)} %fusion.192) | copy-start | bytes 6148
  67.0 74.8 %copy-start.173 = (f32[512]{0:T(512)}, f32[512]{0:T(512)S(1)}, u32[]{:S(2)}) copy-start(f32[512]{0:T(512)S(1)} %fusion.190) | copy-start | bytes 6148
  68.1 131.8 %copy-start.84 = (pred[512,512]{0,1:T(8,128)(4,1)}, pred[512,512]{0,1:T(8,128)(4,1)S(1)}, u32[]{:S(2)}) copy-start(pred[512,512]{0,1:T(8,128)(4,1)S(1)} %fusion.174) | copy-start | bytes 786436
  68.8 234.2 %copy-start.110 = (f32[512]{0:T(512)}, f32[512]{0:T(512)S(1)}, u32[]{:S(2)}) copy-start(f32[512]{0:T(512)S(1)} %fusion.187) | copy-start | bytes 6148
  73.1 229.9 %copy-start.125 = (f32[512]{0:T(512)}, f32[512]{0:T(512)S(1)}, u32[]{:S(2)}) copy-start(f32[512]{0:T(512)S(1)} %get-tuple-element.153) | copy-start | bytes 6148
  73.1 229.9 %copy-start.127 = (f32[512]{0:T(512)}, f32[512]{0:T(512)S(1)}, u32[]{:S(2)}) copy-start(f32[512]{0:T(512)S(1)} %get-tuple-element.154) | copy-start | bytes 6148
  133.5 167.5 %copy-start.119 = (f32[512]{0:T(512)}, f32[512]{0:T(512)S(1)}, u32[]{:S(2)}) copy-start(f32[512]{0:T(512)S(1)} %broadcast_multiply_fusion) | copy-start | bytes 6148
  185.1 116.0 %copy-start.134 = (f32[512]{0:T(512)}, f32[512]{0:T(512)S(1)}, u32[]{:S(2)}) copy-start(f32[512]{0:T(512)S(1)} %broadcast_multiply_fusion.2) | copy-start | bytes 6148
  209.3 91.7 %copy-start.138 = (f32[512]{0:T(512)}, f32[512]{0:T(512)S(1)}, u32[]{:S(2)}) copy-start(f32[512]{0:T(512)S(1)} %broadcast_multiply_fusion.4) | copy-start | bytes 6148
  209.6 91.4 %copy-start.136 = (f32[512]{0:T(512)}, f32[512]{0:T(512)S(1)}, u32[]{:S(2)}) copy-start(f32[512]{0:T(512)S(1)} %fusion.195) | copy-start | bytes 6148
  210.4 90.6 %copy-start.178 = (f32[512]{0:T(512)}, f32[512]{0:T(512)S(1)}, u32[]{:S(2)}) copy-start(f32[512]{0:T(512)S(1)} %fusion.193) | copy-start | bytes 6148
  210.5 90.6 %copy-start.176 = (f32[512]{0:T(512)}, f32[512]{0:T(512)S(1)}, u32[]{:S(2)}) copy-start(f32[512]{0:T(512)S(1)} %fusion.191) | copy-start | bytes 6148
  223.7 36.9 %copy-start.5 = (bf16[4,512,768]{2,1,0:T(8,128)(2,1)S(1)}, bf16[4,512,768]{2,1,0:T(8,128)(2,1)}, u32[]{:S(2)}) copy-start(bf16[4,512,768]{2,1,0:T(8,128)(2,1)} %param.17) | copy-start | bytes 9437188
  573.9 223.6 %reduce-scatter.5.cloned.1.call-start = ((), (), s32[]{:S(2)}) async-start(), calls=%async_computation.8 | async-start | bytes 7299072 | tf_op jit(solution)/shard_map/reduce_scatter | solution.py:298
  606.2 332.6 %reduce-scatter.9.cloned.1.call-start = ((), (), s32[]{:S(2)}) async-start(), calls=%async_computation.10 | async-start | bytes 9732096 | tf_op jit(solution)/shard_map/reduce_scatter | solution.py:298
  643.8 437.3 %reduce-scatter.11.cloned.1.call-start = ((), (), s32[]{:S(2)}) async-start(), calls=%async_computation.11 | async-start | bytes 9732096 | tf_op jit(solution)/shard_map/reduce_scatter | solution.py:298
  (206 other events, 1175.9 us)
Sparse Core Ops, SparseCore 0:
  10.9 62.8 all-gather.4
  76.8 52.9 all-gather.6
  132.7 62.6 all-gather.8
  198.1 62.4 all-gather.10
  574.0 97.8 reduce-scatter.6
  678.9 118.5 reduce-scatter.4
  804.0 134.8 reduce-scatter.8
  946.3 134.7 reduce-scatter.10
where the time goes:
time: 1100 us; the launch traced here: 1090 us
  matrix products  518 us (47%)
  waiting for transfers between devices  345 us (31%)
  blocking collectives  84.6 us (8%)
  local copies, waits for them, and re-layouts  61.3 us (6%)
  other arithmetic  60.5 us (6%)
  between operations  17.5 us (2%)
    reduce_scatter x4, waiting for transfers between devices, on_device(): lax.psum_scatter(totals, ('dp', 'fsdp'), scatter_dimension=0, tiled=True)  291 us
    dot_general x16, matrix products, cross_rows(): lax.dot_general(left, right, (((0,), (0,)), ((), ())), preferred_element_...  119 us
    sub x4, matrix products, backward_row(): weight_grad * smooth_sign - centre  108 us
    unnamed x2, blocking collectives  84.6 us
    dot_general x16, matrix products, back_mult(): lax.dot_general(grad_rows, weight, (((1,), (1,)), ((), ())), preferred_el...  73 us
    dot_general x4, matrix products, backward_row(): jnp.einsum('hqk,qhd->khd', signed.astype(jnp.bfloat16), mixed_grad, prefe...  49.9 us
    dot_general x4, matrix products, forward_row(): jnp.einsum('hqk,khd->qhd', signed.astype(jnp.bfloat16), values_all, prefe...  37.6 us
    slice x16, local copies, waits for them, and re-layouts, split_heads(): merged[:, section * width:(section + 1) * width]  33.7 us
  transfers between devices with their start and end apart: 8, of which 6 were waited for; matrix products, arithmetic and copies ran while one was open for 29% of the time, Pallas kernels for 0%

commit v1 on v0

v1 whole, which is shorter than its diff:
```python
import jax
import jax.numpy as jnp
from jax import lax
from jax.experimental import pallas as pl
from jax.experimental.pallas import tpu as pltpu
from jax.sharding import PartitionSpec as P

HEAD = 64
PAIR = 2 * HEAD
SCALE = HEAD ** (-0.5)
AXES = ("dp", "fsdp")
F32 = jnp.float32
BF16 = jnp.bfloat16
HIDE = -1e30
GELU = 0.7978845608028654


def contract(left, right, left_dim, right_dim):
    return lax.dot_general(
        left, right, (((left_dim,), (right_dim,)), ((), ())), preferred_element_type=F32
    )


def mult(left, right):
    return contract(left, right, 1, 0)


def cross_rows(left, right):
    return contract(left, right, 0, 0)


def back_mult(grad_rows, weight):
    return contract(grad_rows, weight, 1, 1)


def normalize(inputs):
    centred = inputs - jnp.mean(inputs, axis=-1, keepdims=True)
    root = lax.rsqrt(jnp.mean(centred * centred, axis=-1, keepdims=True) + 1e-05)
    return centred * root, root


def norm_back(normed, root, grad, gain):
    scaled = grad * gain
    return root * (
        scaled
        - jnp.mean(scaled, axis=-1, keepdims=True)
        - normed * jnp.mean(scaled * normed, axis=-1, keepdims=True)
    )


def gelu_parts(u):
    smooth = jnp.tanh(GELU * (u + 0.044715 * (u * u * u)))
    slope = 0.5 * (1.0 + smooth) + 0.5 * u * (1.0 - smooth * smooth) * GELU * (
        1.0 + 3 * 0.044715 * u * u
    )
    return 0.5 * u * (1.0 + smooth), slope


def allowed_bias(key_seg, query_seg, row):
    keys = lax.broadcasted_iota(jnp.int32, (row, row), 0)
    queries = lax.broadcasted_iota(jnp.int32, (row, row), 1)
    return jnp.where((key_seg == query_seg) & (keys <= queries), 0.0, HIDE)


def forward_kernel(q_ref, k_ref, v_ref, key_seg, query_seg, mixed_ref, total_ref, bias):
    row = q_ref.shape[0]
    half = row // 2

    @pl.when(pl.program_id(1) == 0)
    def _():
        bias[...] = allowed_bias(key_seg[0], query_seg[0], row)

    lane = lax.broadcasted_iota(jnp.int32, (1, PAIR), 1)
    keys = k_ref[...]
    values = v_ref[...].T
    for part in range(2):
        here = slice(part * half, (part + 1) * half)
        seen = (part + 1) * half
        queries = q_ref[here, :] * jnp.asarray(SCALE, BF16)
        both = []
        for head in range(2):
            own = (lane < HEAD) == (head == 0)
            scores = back_mult(keys[:seen], jnp.where(own, queries, jnp.zeros((), BF16)))
            square = scores * scores + 1.0
            shown = square * lax.rsqrt(square) + bias[:seen, here]
            top = jnp.max(shown, axis=0, keepdims=True)
            weight = jnp.exp(shown - top)
            total = jnp.sum(weight, axis=0, keepdims=True)
            signed = (jnp.tanh(scores) * weight).astype(BF16)
            mixed = mult(values[head * HEAD : (head + 1) * HEAD, :seen], signed)
            both.append(mixed * (1.0 / total))
            total_ref[0, 0, head : head + 1, here] = top + jnp.log(total)
        mixed_ref[here, :] = jnp.concatenate(both, axis=0).T.astype(BF16)


def attention_forward(merged, key_seg, query_seg, row):
    count, width = merged.shape
    model = width // 3
    pairs = model // PAIR
    rows = count // row
    area = rows * pairs * 2 * row * row
    return pl.pallas_call(
        forward_kernel,
        grid=(rows, pairs),
        in_specs=[
            pl.BlockSpec((row, PAIR), lambda r, h: (r, h)),
            pl.BlockSpec((row, PAIR), lambda r, h: (r, h + pairs)),
            pl.BlockSpec((row, PAIR), lambda r, h: (r, h + 2 * pairs)),
            pl.BlockSpec((1, row, 1), lambda r, h: (r, 0, 0)),
            pl.BlockSpec((1, 1, row), lambda r, h: (r, 0, 0)),
        ],
        out_specs=[
            pl.BlockSpec((row, PAIR), lambda r, h: (r, h)),
            pl.BlockSpec((1, 1, 2, row), lambda r, h: (r, h, 0, 0)),
        ],
        out_shape=[
            jax.ShapeDtypeStruct((count, model), BF16),
            jax.ShapeDtypeStruct((rows, pairs, 2, row), F32),
        ],
        scratch_shapes=[pltpu.VMEM((row, row), F32)],
        compiler_params=pltpu.CompilerParams(vmem_limit_bytes=40 * 2**20),
        cost_estimate=pl.CostEstimate(
            flops=area * 4 * HEAD * 6, bytes_accessed=count * width * 3, transcendentals=area * 3
        ),
        name="attention_forward",
    )(merged, merged, merged, key_seg, query_seg)


def backward_kernel(
    q_ref, k_ref, v_ref, mixed_ref, grad_ref, total_ref, key_seg, query_seg, dq_ref, dk_ref, dv_ref, bias
):
    row = q_ref.shape[0]
    half = row // 2

    @pl.when(pl.program_id(1) == 0)
    def _():
        bias[...] = allowed_bias(key_seg[0], query_seg[0], row)

    lane = lax.broadcasted_iota(jnp.int32, (1, PAIR), 1)
    keys = k_ref[...]
    values = v_ref[...]
    turned = keys.T
    key_grads = [jnp.zeros((half, PAIR), F32) for _ in range(2)]
    value_grads = [jnp.zeros((half, PAIR), F32) for _ in range(2)]
    for part in range(2):
        here = slice(part * half, (part + 1) * half)
        seen = (part + 1) * half
        queries = q_ref[here, :] * jnp.asarray(SCALE, BF16)
        grads = grad_ref[here, :]
        centres = (grads.astype(F32) * mixed_ref[here, :].astype(F32)).T
        both = []
        for head in range(2):
            span = slice(head * HEAD, (head + 1) * HEAD)
            own = (lane < HEAD) == (head == 0)
            head_queries = jnp.where(own, queries, jnp.zeros((), BF16))
            head_grads = jnp.where(own, grads, jnp.zeros((), BF16))
            centre = jnp.sum(centres[span], axis=0, keepdims=True)
            scores = back_mult(keys[:seen], head_queries)
            weight_grad = back_mult(values[:seen], head_grads)
            square = scores * scores + 1.0
            root = lax.rsqrt(square)
            weight = jnp.exp(
                square * root + (bias[:seen, here] - total_ref[0, 0, head : head + 1, here])
            )
            smooth = jnp.tanh(scores)
            signed = (smooth * weight).astype(BF16)
            bent = weight_grad * smooth
            score_grad = weight * (
                (weight_grad - bent * smooth) + (scores * root) * (bent - centre)
            )
            score_grad = score_grad.astype(BF16)
            value_part = mult(signed, head_grads)
            key_part = mult(score_grad, head_queries)
            for block in range(part + 1):
                rows = slice(block * half, (block + 1) * half)
                value_grads[block] = value_grads[block] + value_part[rows]
                key_grads[block] = key_grads[block] + key_part[rows]
            both.append(mult(turned[span, :seen], score_grad))
        dq_ref[here, :] = (jnp.concatenate(both, axis=0).T * SCALE).astype(BF16)
    for block in range(2):
        rows = slice(block * half, (block + 1) * half)
        dk_ref[rows, :] = key_grads[block].astype(BF16)
        dv_ref[rows, :] = value_grads[block].astype(BF16)


def attention_backward(merged, mixed, mixed_grad, total, key_seg, query_seg, row):
    count, width = merged.shape
    model = width // 3
    pairs = model // PAIR
    rows = count // row
    area = rows * pairs * 2 * row * row
    block = pl.BlockSpec((row, PAIR), lambda r, h: (r, h))
    return pl.pallas_call(
        backward_kernel,
        grid=(rows, pairs),
        in_specs=[
            block,
            pl.BlockSpec((row, PAIR), lambda r, h: (r, h + pairs)),
            pl.BlockSpec((row, PAIR), lambda r, h: (r, h + 2 * pairs)),
            block,
            block,
            pl.BlockSpec((1, 1, 2, row), lambda r, h: (r, h, 0, 0)),
            pl.BlockSpec((1, row, 1), lambda r, h: (r, 0, 0)),
            pl.BlockSpec((1, 1, row), lambda r, h: (r, 0, 0)),
        ],
        out_specs=[block, block, block],
        out_shape=[jax.ShapeDtypeStruct((count, model), BF16)] * 3,
        scratch_shapes=[pltpu.VMEM((row, row), F32)],
        compiler_params=pltpu.CompilerParams(vmem_limit_bytes=40 * 2**20),
        cost_estimate=pl.CostEstimate(
            flops=area * 10 * HEAD * 4, bytes_accessed=count * width * 5, transcendentals=area * 3
        ),
        name="attention_backward",
    )(merged, merged, merged, mixed, mixed_grad, total, key_seg, query_seg)


class Links:
    def __init__(self, mesh):
        self.outer = mesh.shape["dp"]
        self.inner = mesh.shape["fsdp"]
        self.count = self.outer * self.inner
        self.far = [(k << 2) * self.inner for k in range(self.outer // 4)]
        self.near = [(b << 1) * self.inner + f for b in range(2) for f in range(self.inner)]
        self.core = self.inner

    def place(self):
        return lax.axis_index("dp") * self.inner + lax.axis_index("fsdp")

    def swap(self, piece, mask):
        return lax.ppermute(piece, AXES, [(i, i ^ mask) for i in range(self.count)])

    def spread(self, shard):
        column = jnp.stack([shard] + [self.swap(shard, mask) for mask in self.far[1:]])
        plane = [column] + [self.swap(column, mask) for mask in self.near[1:]]
        return plane + [self.swap(piece, self.core) for piece in plane]

    def arrange(self, pieces, columns):
        masks = self.near + [mask ^ self.core for mask in self.near]
        far = self.far
        held = len(pieces)
        rows = pieces[0].shape[1]

        def kernel(me_ref, *refs):
            targets, sem = refs[held:-1], refs[-1]
            me = me_ref[0]
            copies = []
            for piece, mask in zip(refs[:held], masks):
                for k, step in enumerate(far):
                    owner = jnp.bitwise_xor(me, mask ^ step)
                    for target, (start, width, parts) in zip(targets, columns):
                        for part in range(parts):
                            copies.append(
                                pltpu.make_async_copy(
                                    piece.at[k, :, pl.ds(start + part * width, width)],
                                    target.at[owner * parts + part],
                                    sem,
                                )
                            )
            for copy in copies:
                copy.start()
            for copy in copies:
                copy.wait()

        return pl.pallas_call(
            kernel,
            in_specs=[pl.BlockSpec(memory_space=pltpu.SMEM)]
            + [pl.BlockSpec(memory_space=pl.ANY)] * held,
            out_specs=[pl.BlockSpec(memory_space=pltpu.VMEM)] * len(columns),
            out_shape=[
                jax.ShapeDtypeStruct((self.count * parts, rows, width), BF16)
                for _, width, parts in columns
            ],
            scratch_shapes=[pltpu.SemaphoreType.DMA],
            compiler_params=pltpu.CompilerParams(vmem_limit_bytes=40 * 2**20),
            name="arrange",
        )(jnp.full((1,), self.place(), jnp.int32), *pieces)

    def reduce(self, grads, join):
        dp = lax.axis_index("dp")
        core, side, column, inner = dp & 1, (dp >> 1) & 1, dp >> 2, lax.axis_index("fsdp")

        def pick(array, index, axis):
            return lax.dynamic_index_in_dim(array, index, axis, keepdims=False)

        views = [
            grad.reshape((self.outer // 4, 2, 2, self.inner) + grad.shape[1:]) for grad in grads
        ]
        got = [self.swap(pick(view, 1 - core, 2), self.core) for view in views]
        mine = [pick(view, core, 2) for view in views]
        sums = []
        for b in range(2):
            for f in range(self.inner):

                def cut(array):
                    return pick(pick(array, side ^ b, 1), inner ^ f, 1).astype(F32)

                sums.append(join([(cut(a) + cut(b)).astype(BF16) for a, b in zip(mine, got)]))
        sums = sums[:1] + [self.swap(part, mask) for part, mask in zip(sums[1:], self.near[1:])]
        result = None
        for k, mask in enumerate(self.far):
            part = sum(pick(array, column ^ k, 0).astype(F32) for array in sums)
            if k == 0:
                result = part
            else:
                result = result + self.swap(part.astype(BF16), mask).astype(F32)
        return result


def run(
    links,
    tokens,
    lengths,
    cotangent,
    attn_norm_gain,
    attn_norm_bias,
    qkv_weight,
    qkv_bias,
    out_weight,
    out_bias,
    mlp_norm_gain,
    mlp_norm_bias,
    up_weight,
    up_bias,
    down_weight,
    down_bias,
):
    micro, row, model = tokens.shape
    count = micro * row
    shard = qkv_weight.shape[0]
    wide = up_weight.shape[1]
    wide_parts = wide // model
    devices = links.count

    vectors = (
        attn_norm_gain,
        attn_norm_bias,
        qkv_bias,
        out_bias,
        mlp_norm_gain,
        mlp_norm_bias,
        up_bias,
        down_bias,
    )
    extra = jnp.concatenate([vector.reshape(shard, -1) for vector in vectors], axis=1)
    extra = jnp.pad(extra, ((0, 0), (0, PAIR - extra.shape[1])))
    first_pieces = links.spread(jnp.concatenate([qkv_weight, extra], axis=1))
    rest = jnp.concatenate(
        [out_weight, up_weight]
        + [down_weight[part * shard : (part + 1) * shard] for part in range(wide_parts)],
        axis=1,
    )
    rest_pieces = links.spread(rest)
    full_qkv, full_extra = links.arrange(first_pieces, [(0, 3 * model, 1), (3 * model, PAIR, 1)])
    full_qkv = full_qkv.reshape(model, 3 * model)
    full_extra = full_extra.reshape(model, PAIR).T.astype(F32)
    full_vectors = []
    at = 0
    for vector in vectors:
        parts = vector.shape[0] // shard
        full_vectors.append(full_extra[at : at + parts].T.reshape(1, -1))
        at += parts
    gain_one, bias_one, bias_qkv, bias_out, gain_two, bias_two, bias_up, bias_down = full_vectors

    ends = jnp.cumsum(lengths.reshape(micro, -1), axis=1, dtype=jnp.int32)
    places = jnp.arange(row, dtype=jnp.int32)
    segment = jnp.sum((ends[:, None, :] <= places[None, :, None]).astype(jnp.int32), axis=2)
    valid = (places[None, :] < ends[:, -1:]).reshape(count, 1)
    key_seg, query_seg = segment[:, :, None], segment[:, None, :]

    residual = tokens.reshape(count, model).astype(F32)
    unit_one, root_one = normalize(residual)
    normed_one = (unit_one * gain_one + bias_one).astype(BF16)
    merged = (mult(normed_one, full_qkv) + bias_qkv).astype(BF16)
    mixed, log_total = attention_forward(merged, key_seg, query_seg, row)

    full_out, full_up, full_down = links.arrange(
        rest_pieces, [(0, model, 1), (model, wide, 1), (model + wide, model, wide_parts)]
    )
    full_out = full_out.reshape(model, model)
    full_up = full_up.reshape(model, wide)
    full_down = full_down.reshape(wide, model)

    hidden = residual + mult(mixed, full_out) + bias_out
    unit_two, root_two = normalize(hidden)
    normed_two = (unit_two * gain_two + bias_two).astype(BF16)
    pre_act = mult(normed_two, full_up) + bias_up
    activated, slope = gelu_parts(pre_act)
    activated = activated.astype(BF16)
    block_out = (hidden + mult(activated, full_down) + bias_down).astype(BF16)

    down_grad = jnp.where(valid, cotangent.reshape(count, model), jnp.zeros((), BF16))
    out_grad = down_grad.astype(F32)
    grad_down = cross_rows(activated, down_grad)
    grad_bias_down = jnp.sum(out_grad, axis=0)
    up_grad = (slope * back_mult(down_grad, full_down)).astype(BF16)
    grad_up = cross_rows(normed_two, up_grad)
    grad_bias_up = jnp.sum(up_grad.astype(F32), axis=0)
    normed_grad = back_mult(up_grad, full_up)
    grad_gain_two = jnp.sum(normed_grad * unit_two, axis=0)
    grad_bias_two = jnp.sum(normed_grad, axis=0)
    hidden_grad = out_grad + norm_back(unit_two, root_two, normed_grad, gain_two)
    proj_grad = hidden_grad.astype(BF16)
    grad_out = cross_rows(mixed, proj_grad)
    grad_bias_out = jnp.sum(proj_grad.astype(F32), axis=0)

    late = links.reduce(
        [
            grad_out.astype(BF16).reshape(devices, shard, model),
            grad_up.astype(BF16).reshape(devices, shard, wide),
            grad_down.astype(BF16).reshape(devices, wide_parts * shard, model),
        ],
        lambda cuts: jnp.concatenate(
            [cuts[0], cuts[2]]
            + [cuts[1][:, :, part * model : (part + 1) * model] for part in range(wide_parts)],
            axis=1,
        ),
    )
    out_shard = late[:shard]
    down_shard = late[shard : shard * (1 + wide_parts)]
    up_shard = late[shard * (1 + wide_parts) :].reshape(wide_parts, shard, model)
    up_shard = jnp.concatenate([up_shard[part] for part in range(wide_parts)], axis=1)

    mixed_grad = back_mult(proj_grad, full_out).astype(BF16)
    merged_grad = jnp.concatenate(
        attention_backward(merged, mixed, mixed_grad, log_total, key_seg, query_seg, row), axis=1
    )
    grad_qkv = cross_rows(normed_one, merged_grad)
    grad_bias_qkv = jnp.sum(merged_grad.astype(F32), axis=0)
    first_grad = back_mult(merged_grad, full_qkv)
    grad_gain_one = jnp.sum(first_grad * unit_one, axis=0)
    grad_bias_one = jnp.sum(first_grad, axis=0)
    token_grad = (hidden_grad + norm_back(unit_one, root_one, first_grad, gain_one)).astype(BF16)

    sums = (
        grad_gain_one,
        grad_bias_one,
        grad_bias_qkv,
        grad_bias_out,
        grad_gain_two,
        grad_bias_two,
        grad_bias_up,
        grad_bias_down,
    )
    tail = jnp.concatenate([total.reshape(model, -1) for total in sums], axis=1)
    tail = jnp.pad(tail, ((0, 0), (0, PAIR - tail.shape[1])))
    last = links.reduce(
        [
            grad_qkv.astype(BF16).reshape(devices, shard, 3 * model),
            tail.astype(BF16).reshape(devices, shard, PAIR),
        ],
        lambda cuts: jnp.concatenate(cuts, axis=2),
    )
    parts = []
    at = 3 * model
    for vector in vectors:
        width = vector.shape[0] // shard
        parts.append(last[:, at : at + width].reshape(-1))
        at += width
    (
        gain_one_shard,
        bias_one_shard,
        bias_qkv_shard,
        bias_out_shard,
        gain_two_shard,
        bias_two_shard,
        bias_up_shard,
        bias_down_shard,
    ) = parts
    return (
        block_out.reshape(tokens.shape),
        token_grad.reshape(tokens.shape),
        gain_one_shard,
        bias_one_shard,
        last[:, : 3 * model],
        bias_qkv_shard,
        out_shard,
        bias_out_shard,
        gain_two_shard,
        bias_two_shard,
        up_shard,
        bias_up_shard,
        down_shard,
        bias_down_shard,
    )


def solution(mesh):
    links = Links(mesh)
    rows = P(None, AXES, None)
    vector = P(AXES)
    matrix = P(AXES, None)
    params = (
        vector,
        vector,
        matrix,
        vector,
        matrix,
        vector,
        vector,
        vector,
        matrix,
        vector,
        matrix,
        vector,
    )
    return jax.shard_map(
        lambda *args: run(links, *args),
        mesh=mesh,
        in_specs=(rows, rows, rows) + params,
        out_specs=(rows, rows) + params,
        check_vma=False,
    )
```

time: 1100 us -> 538 us (0.49)
  matrix products: 518 us -> 164 us
  waiting for transfers between devices: 345 us -> 128 us
  Pallas kernels: 0 us -> 104 us
  blocking collectives: 84.6 us -> 0 us
  starting transfers between devices: 0.89 us -> 34.4 us
  between operations: 17.5 us -> 1.74 us
  other arithmetic: 60.5 us -> 45.7 us
    reduce_scatter x4 -> x0, waiting for transfers between devices: 291 us -> none  [on_device(): lax.psum_scatter(totals, ('dp', 'fsdp'), scatter_dimension=0, tiled=True)]
    dot_general x68 -> x12, matrix products: 410 us -> 164 us  [contract(): lax.dot_general(left, right, (((left_dim,), (right_dim,)), ((), ())), pre...]
    ppermute x0 -> x37, waiting for transfers between devices: none -> 128 us  [swap(): return lax.ppermute(piece, AXES, [(i, i ^ mask) for i in range(self.count)])]
    sub x4 -> x0, matrix products: 108 us -> none  [backward_row(): weight_grad * smooth_sign - centre]
    pallas_call x0 -> x4, Pallas kernels: none -> 104 us  [the longest x1 51.2 us: attention_backward(): pl.pallas_call(backward_kernel, grid=(rows, pairs), in_specs=[block, pl.B...]
    unnamed x2 -> x0, blocking collectives: 84.6 us -> none
    all_gather x4 -> x0, waiting for transfers between devices: 51.4 us -> none  [the longest x1 32.1 us: on_device(): lax.all_gather(shards[10], ('dp', 'fsdp'), axis=0, tiled=True)]
    ppermute x0 -> x37, starting transfers between devices: none -> 34.4 us  [swap(): return lax.ppermute(piece, AXES, [(i, i ^ mask) for i in range(self.count)])]
  transfers between devices with their start and end apart: 8 -> 37, of which waited for: 6 -> 11; matrix products, arithmetic and copies ran while one was open for 29% -> 26% of each run, Pallas kernels for 0% -> 18%
where the time goes in v1:
time: 538 us; the launch traced here: 532 us
  matrix products  164 us (30%)
  waiting for transfers between devices  128 us (24%)
  Pallas kernels  104 us (19%)
  local copies, waits for them, and re-layouts  54.5 us (10%)
  other arithmetic  45.7 us (8%)
  starting transfers between devices  34.4 us (6%)
    dot_general x12, matrix products, contract(): lax.dot_general(left, right, (((left_dim,), (right_dim,)), ((), ())), pre...  164 us
    ppermute x37, waiting for transfers between devices, swap(): return lax.ppermute(piece, AXES, [(i, i ^ mask) for i in range(self.count)])  128 us
    pallas_call x1, Pallas kernels, attention_backward(): pl.pallas_call(backward_kernel, grid=(rows, pairs), in_specs=[block, pl.B...  51.2 us
    pallas_call x1, Pallas kernels, attention_forward(): pl.pallas_call(forward_kernel, grid=(rows, pairs), in_specs=[pl.BlockSpec...  44.4 us
    ppermute x37, starting transfers between devices, swap(): return lax.ppermute(piece, AXES, [(i, i ^ mask) for i in range(self.count)])  34.4 us
    unnamed x110, local copies, waits for them, and re-layouts  19.1 us
  transfers between devices with their start and end apart: 37, of which 11 were waited for; matrix products, arithmetic and copies ran while one was open for 26% of the time, Pallas kernels for 18%

profile of v1, /device:TPU:0, one launch (start us, length us, event | category | flops | bytes accessed | tf_op | source)
XLA Modules:
  0.0 532.3 jit_solution(5380867313059678154)
XLA Ops:
  8.5 4.0 collective-permute-start.1
  40.5 3.7 fusion.80
  46.4 7.1 %collective-permute-done.5.refs_3_ = bf16[4,24,2432]{2,1,0:T(8,128)(2,1)} collective-permute-done((bf16[4,24,2432]{2,1,0:T(8,128)(2,1)S(1)}, bf16[4,24,2432]{2,1,0:T(8,128)(2,1)}, u32[]{:S(2)}, u32[]{:S(2)}) %collective-permute-start.5) | collective-permute-done | bytes 466976 | tf_op jit(solution)/shard_map/ppermute | solution.py:230
  63.5 2.9 fusion.14
  66.5 7.9 %add_convert_fusion.q_ref.k_ref.v_ref = bf16[2048,2304]{1,0:T(8,128)(2,1)S(1)} fusion(bf16[2048,768]{1,0:T(8,128)(2,1)S(1)} %bitcast.314, bf16[768,2304]{1,0:T(8,128)(2,1)S(1)} %bitcast.294, f32[2304]{0:T(1024)S(1)} %add.751), kind=kOutput, calls=%fused_computation.12 | convolution fusion | flops 7257194496 | bytes 16131072 | tf_op jit(solution)/shard_map/dot_general | solution.py:19
  74.4 12.0 %collective-permute-done.13.refs_1_ = bf16[4,24,6912]{2,1,0:T(8,128)(2,1)S(1)} collective-permute-done((bf16[4,24,6912]{2,1,0:T(8,128)(2,1)S(1)}, bf16[4,24,6912]{2,1,0:T(8,128)(2,1)S(1)}, u32[]{:S(2)}, u32[]{:S(2)}) %collective-permute-start.13) | collective-permute-done | bytes 1327136 | tf_op jit(solution)/shard_map/ppermute | solution.py:230
  88.5 27.7 %collective-permute-done.15.refs_3_ = bf16[4,24,6912]{2,1,0:T(8,128)(2,1)} collective-permute-done((bf16[4,24,6912]{2,1,0:T(8,128)(2,1)S(1)}, bf16[4,24,6912]{2,1,0:T(8,128)(2,1)}, u32[]{:S(2)}, u32[]{:S(2)}) %collective-permute-start.15) | collective-permute-done | bytes 1327136 | tf_op jit(solution)/shard_map/ppermute | solution.py:230
  116.2 44.4 %attention_forward.1 = (bf16[2048,768]{1,0:T(8,128)(2,1)S(1)}, f32[4,6,2,512]{3,2,1,0:T(2,128)S(1)}) custom-call(bf16[2048,2304]{1,0:T(8,128)(2,1)S(1)} %add_convert_fusion.q_ref.k_ref.v_ref, bf16[2048,2304]{1,0:T(8,128)(2,1)S(1)} %add_convert_fusion.q_ref.k_ref.v_ref, bf16[2048,2304]{1,0:T(8,128)(2,1)S(1)} %add_convert_fusion.q_ref.k_ref.v_ref, ...), custom_call_target="tpu_custom_call" | custom-call | flops 19327352832 | bytes 14155776 | tf_op jit(solution)/shard_map/attention_forward/pallas_call | solution.py:102
  160.7 6.9 %arrange.3 = (bf16[32,24,768]{2,1,0:T(8,128)(2,1)S(1)}, bf16[32,24,3072]{2,1,0:T(8,128)(2,1)}, bf16[128,24,768]{2,1,0:T(8,128)(2,1)}) custom-call(s32[1]{0:T(128)} %bitcast.1.me_ref, bf16[4,24,6912]{2,1,0:T(8,128)(2,1)S(1)} %pad_maximum_fusion.refs_0_, bf16[4,24,6912]{2,1,0:T(8,128)(2,1)S(1)} %collective-permute-done.13.refs_1_, ...), custom_call_target="tpu_custom_call" | custom-call | tf_op jit(solution)/shard_map/arrange/pallas_call | solution.py:264
  167.6 4.6 fusion.82
  172.2 3.6 multiply_reduce_fusion.2
  175.9 22.9 %multiply_convert_fusion = (bf16[2048,3072]{1,0:T(8,128)(2,1)}, f32[2048,3072]{1,0:T(8,128)}) fusion(f32[3072]{0:T(1024)S(1)} %add.762, bf16[768,3072]{1,0:T(8,128)(2,1)S(1)} %bitcast.345, f32[2048,768]{1,0:T(8,128)} %get-tuple-element.100, f32[768]{0:T(1024)S(1)} %get-tuple-element.43, f32[768]{0:T(1024)S(1)} %get-tuple-element.44, ...), kind=kOutput, calls=%fused_computation.11 | convolution fusion | flops 9734455296 | bytes 48793600 | tf_op jit(solution)/shard_map/dot_general | solution.py:19
  198.7 28.2 %fusion.83 = (bf16[3072]{0:T(1024)(128)(2,1)}, bf16[2048,3072]{1,0:T(8,128)(2,1)}) fusion(bf16[2048,768]{1,0:T(8,128)(2,1)S(1)} %bitcast.315, bf16[3072,768]{1,0:T(8,128)(2,1)} %bitcast.340, f32[2048,3072]{1,0:T(8,128)} %get-tuple-element.102, f32[3072]{0:T(1024)S(1)} %add.762), kind=kOutput, calls=%fused_computation.213 | convolution fusion | flops 9795793920 | bytes 45631488 | tf_op jit(solution)/shard_map/dot_general | solution.py:19
  226.9 18.4 %convolution_convert_fusion = bf16[768,3072]{1,0:T(8,128)(2,1)} fusion(bf16[2048,3072]{1,0:T(8,128)(2,1)} %get-tuple-element.106, f32[2048,768]{1,0:T(8,128)} %get-tuple-element.100, f32[768]{0:T(1024)S(1)} %get-tuple-element.43, f32[768]{0:T(1024)S(1)} %get-tuple-element.44, f32[2048]{0:T(1024)S(1)} %add_rsqrt_fusion, f32[2048]{0:T(1024)S(1)} %broadcast_multiply_fusion.4), kind=kOutput, calls=%fused_computation.46 | convolution fusion | flops 9673900032 | bytes 23615488 | tf_op jit(solution)/shard_map/dot_general | solution.py:19
  245.3 18.7 %multiply_reduce_fusion = (bf16[768]{0:T(1024)(128)(2,1)}, f32[2048]{0:T(1024)S(1)}, f32[2048]{0:T(1024)S(1)}, bf16[768]{0:T(1024)(128)(2,1)}, f32[2048,768]{1,0:T(8,128)}) fusion(f32[2048,768]{1,0:T(8,128)} %get-tuple-element.100, f32[2048]{0:T(1024)S(1)} %add_rsqrt_fusion, f32[2048]{0:T(1024)S(1)} %broadcast_multiply_fusion.4, ...), kind=kOutput, calls=%fused_computation.37 | convolution fusion | flops 9677826048 | bytes 29923328 | tf_op jit(solution)/shard_map/dot_general | solution.py:19
  264.1 6.6 %convert_reduce_fusion.2 = (bf16[768]{0:T(1024)(128)(2,1)S(1)}, f32[2048,768]{1,0:T(8,128)S(1)}, bf16[2048,768]{1,0:T(8,128)(2,1)S(1)}) fusion(f32[2048]{0:T(1024)S(1)} %get-tuple-element.107, f32[2048,768]{1,0:T(8,128)} %get-tuple-element.100, f32[2048]{0:T(1024)S(1)} %broadcast_multiply_fusion.4, f32[2048]{0:T(1024)S(1)} %get-tuple-element.108, ...), kind=kLoop, calls=%fused_computation.203 | loop fusion | flops 18873600 | bytes 25205248 | tf_op jit(solution)/shard_map/reduce_sum | solution.py:404
  270.7 2.8 convolution_convert_fusion.4
  273.9 4.0 convolution_convert_fusion.3.grad_ref
  280.1 13.2 %convolution_convert_fusion.1 = bf16[3072,768]{1,0:T(8,128)(2,1)S(1)} fusion(bf16[2048,3072]{1,0:T(8,128)(2,1)} %get-tuple-element.101, bf16[2048,768]{1,0:T(8,128)(2,1)S(1)} %get-tuple-element.58), kind=kOutput, calls=%fused_computation.47 | convolution fusion | flops 9666035712 | bytes 20447232 | tf_op jit(solution)/shard_map/dot_general | solution.py:19
  296.5 51.2 %attention_backward.1 = (bf16[2048,768]{1,0:T(8,128)(2,1)S(1)}, bf16[2048,768]{1,0:T(8,128)(2,1)S(1)}, bf16[2048,768]{1,0:T(8,128)(2,1)S(1)}) custom-call(bf16[2048,2304]{1,0:T(8,128)(2,1)} %copy-done.5, bf16[2048,2304]{1,0:T(8,128)(2,1)} %copy-done.5, bf16[2048,2304]{1,0:T(8,128)(2,1)} %copy-done.5, bf16[2048,768]{1,0:T(8,128)(2,1)S(1)} %get-tuple-element.26.mixed_ref, ...), custom_call_target="tpu_custom_call" | custom-call | flops 32212254720 | bytes 23592960 | tf_op jit(solution)/shard_map/attention_backward/pallas_call | solution.py:193
  355.1 14.3 %fusion.28 = (bf16[768]{0:T(1024)(128)(2,1)S(1)}, f32[2048]{0:T(1024)}, f32[2048]{0:T(1024)}, bf16[768]{0:T(1024)(128)(2,1)S(1)}, bf16[2048,768]{1,0:T(8,128)(2,1)}, /*index=5*/f32[2048,768]{1,0:T(8,128)}) fusion(bf16[4,512,768]{2,1,0:T(8,128)(2,1)S(1)} %copy-done.8, f32[2048]{0:T(1024)S(1)} %bitcast.330, f32[2048]{0:T(1024)S(1)} %bitcast.328, ...), kind=kOutput, calls=%fused_computation.36 | convolution fusion | flops 7268198400 | bytes 25601024 | tf_op jit(solution)/shard_map/dot_general | solution.py:19
  370.4 5.7 %reduce.3 = bf16[2304]{0:T(1024)(128)(2,1)} reduce(bf16[2048,2304]{1,0:T(8,128)(2,1)} %constant_dynamic-update-slice_fusion.6, bf16[]{:T(256)} %constant.1658.clone.1), dimensions={0}, to_apply=%region_12.13.clone | reduce | flops 4716288 | bytes 9441794 | tf_op jit(solution)/shard_map/reduce_sum | solution.py:428
  387.4 12.1 %convolution_convert_fusion.2 = bf16[768,2304]{1,0:T(8,128)(2,1)S(1)} fusion(bf16[2048,768]{1,0:T(8,128)(2,1)} %get-tuple-element.74, bf16[2048,2304]{1,0:T(8,128)(2,1)} %constant_dynamic-update-slice_fusion.6), kind=kOutput, calls=%fused_computation.48 | convolution fusion | flops 7249526784 | bytes 16121856 | tf_op jit(solution)/shard_map/dot_general | solution.py:19
  400.2 16.6 %add_convert_fusion.1 = bf16[2048,768]{1,0:T(8,128)(2,1)} fusion(f32[2048,768]{1,0:T(8,128)} %get-tuple-element.100, bf16[2048,3072]{1,0:T(8,128)(2,1)} %get-tuple-element.101, bf16[3072,768]{1,0:T(8,128)(2,1)} %bitcast.341, f32[768]{0:T(1024)S(1)} %copy-done.30), kind=kOutput, calls=%fused_computation.40 | convolution fusion | flops 9668395008 | bytes 26741760 | tf_op jit(solution)/shard_map/dot_general | solution.py:19
  423.4 2.6 fusion.35
  426.0 3.7 fusion.43
  436.3 3.4 fusion.25
  439.7 5.2 collective-permute-done.24
  447.2 25.6 %collective-permute-done.31 = bf16[4,216,768]{2,1,0:T(8,128)(2,1)S(1)} collective-permute-done((bf16[4,216,768]{2,1,0:T(8,128)(2,1)}, bf16[4,216,768]{2,1,0:T(8,128)(2,1)S(1)}, u32[]{:S(2)}, u32[]{:S(2)}) %collective-permute-start.31) | collective-permute-done | bytes 1327136 | tf_op jit(solution)/shard_map/ppermute | solution.py:230
  474.0 26.5 %collective-permute-done.33 = bf16[4,216,768]{2,1,0:T(8,128)(2,1)S(1)} collective-permute-done((bf16[4,216,768]{2,1,0:T(8,128)(2,1)S(1)}, bf16[4,216,768]{2,1,0:T(8,128)(2,1)S(1)}, u32[]{:S(2)}, u32[]{:S(2)}) %collective-permute-start.33) | collective-permute-done | bytes 1327136 | tf_op jit(solution)/shard_map/ppermute | solution.py:230
  508.5 6.8 %collective-permute-done.34 = bf16[216,768]{1,0:T(8,128)(2,1)S(1)} collective-permute-done((bf16[216,768]{1,0:T(8,128)(2,1)S(1)}, bf16[216,768]{1,0:T(8,128)(2,1)S(1)}, u32[]{:S(2)}, u32[]{:S(2)}) %collective-permute-start.34) | collective-permute-done | bytes 331808 | tf_op jit(solution)/shard_map/ppermute | solution.py:230
  515.3 13.0 %collective-permute-done.35 = bf16[216,768]{1,0:T(8,128)(2,1)S(1)} collective-permute-done((bf16[216,768]{1,0:T(8,128)(2,1)S(1)}, bf16[216,768]{1,0:T(8,128)(2,1)S(1)}, u32[]{:S(2)}, u32[]{:S(2)}) %collective-permute-start.35) | collective-permute-done | bytes 331808 | tf_op jit(solution)/shard_map/ppermute | solution.py:230
  (258 shorter events, 104.2 us)
Async XLA Ops:
  8.5 21.5 %collective-permute-start.1 = (bf16[24,2432]{1,0:T(8,128)(2,1)}, bf16[24,2432]{1,0:T(8,128)(2,1)S(1)}, u32[]{:S(2)}, u32[]{:S(2)}) collective-permute-start(bf16[24,2432]{1,0:T(8,128)(2,1)} %get-tuple-element.92), channel_id=1, source_target_pairs={{0,16},{1,17},{2,18},{3,19},{4,20},{5,21},{6,22},{7,23},{8,24},{9,... | collective-permute-start | bytes 350216 | tf_op jit(solution)/shard_map/ppermute | solution.py:230
  12.6 17.5 %collective-permute-start.2 = (bf16[24,2432]{1,0:T(8,128)(2,1)}, bf16[24,2432]{1,0:T(8,128)(2,1)S(1)}, u32[]{:S(2)}, u32[]{:S(2)}) collective-permute-start(bf16[24,2432]{1,0:T(8,128)(2,1)} %get-tuple-element.92), channel_id=1, source_target_pairs={{0,24},{1,25},{2,26},{3,27},{4,28},{5,29},{6,30},{7,31},{8,16},{9,... | collective-permute-start | bytes 350216 | tf_op jit(solution)/shard_map/ppermute | solution.py:230
  13.9 16.2 %collective-permute-start = (bf16[24,2432]{1,0:T(8,128)(2,1)}, bf16[24,2432]{1,0:T(8,128)(2,1)}, u32[]{:S(2)}, u32[]{:S(2)}) collective-permute-start(bf16[24,2432]{1,0:T(8,128)(2,1)} %get-tuple-element.92), channel_id=1, source_target_pairs={{0,8},{1,9},{2,10},{3,11},{4,12},{5,13},{6,14},{7,15},{8,0},{9,1},... | collective-permute-start | bytes 350216 | tf_op jit(solution)/shard_map/ppermute | solution.py:230
  22.7 16.3 %collective-permute-start.10 = (bf16[24,6912]{1,0:T(8,128)(2,1)}, bf16[24,6912]{1,0:T(8,128)(2,1)}, u32[]{:S(2)}, u32[]{:S(2)}) collective-permute-start(bf16[24,6912]{1,0:T(8,128)(2,1)} %constant_dynamic-update-slice_fusion), channel_id=1, source_target_pairs={{0,8},{1,9},{2,10},{3,11},{4,12},{5,13},{6,14},{7,15},{8,0},{9,1},... | collective-permute-start | bytes 995336 | tf_op jit(solution)/shard_map/ppermute | solution.py:230
  24.5 20.6 %collective-permute-start.11 = (bf16[24,6912]{1,0:T(8,128)(2,1)}, bf16[24,6912]{1,0:T(8,128)(2,1)}, u32[]{:S(2)}, u32[]{:S(2)}) collective-permute-start(bf16[24,6912]{1,0:T(8,128)(2,1)} %constant_dynamic-update-slice_fusion), channel_id=1, source_target_pairs={{0,16},{1,17},{2,18},{3,19},{4,20},{5,21},{6,22},{7,23},{8,24},{9,... | collective-permute-start | bytes 995336 | tf_op jit(solution)/shard_map/ppermute | solution.py:230
  31.1 13.9 %collective-permute-start.3 = (bf16[4,24,2432]{2,1,0:T(8,128)(2,1)S(1)}, bf16[4,24,2432]{2,1,0:T(8,128)(2,1)}, u32[]{:S(2)}, u32[]{:S(2)}) collective-permute-start(bf16[4,24,2432]{2,1,0:T(8,128)(2,1)S(1)} %pad_maximum_fusion.1.refs_0_), channel_id=1, source_target_pairs={{0,1},{1,0},{2,3},{3,2},{4,5},{5,4},{6,7},{7,6},{8,9},{9,8},{10,11... | collective-permute-start | bytes 1400840 | tf_op jit(solution)/shard_map/ppermute | solution.py:230
  34.1 19.3 %collective-permute-start.5 = (bf16[4,24,2432]{2,1,0:T(8,128)(2,1)S(1)}, bf16[4,24,2432]{2,1,0:T(8,128)(2,1)}, u32[]{:S(2)}, u32[]{:S(2)}) collective-permute-start(bf16[4,24,2432]{2,1,0:T(8,128)(2,1)S(1)} %pad_maximum_fusion.1.refs_0_), channel_id=1, source_target_pairs={{0,5},{1,4},{2,7},{3,6},{4,1},{5,0},{6,3},{7,2},{8,13},{9,12},{10,... | collective-permute-start | bytes 1400840 | tf_op jit(solution)/shard_map/ppermute | solution.py:230
  38.9 14.5 %collective-permute-start.12 = (bf16[24,6912]{1,0:T(8,128)(2,1)}, bf16[24,6912]{1,0:T(8,128)(2,1)S(1)}, u32[]{:S(2)}, u32[]{:S(2)}) collective-permute-start(bf16[24,6912]{1,0:T(8,128)(2,1)} %constant_dynamic-update-slice_fusion), channel_id=1, source_target_pairs={{0,24},{1,25},{2,26},{3,27},{4,28},{5,29},{6,30},{7,31},{8,16},{9,... | collective-permute-start | bytes 995336 | tf_op jit(solution)/shard_map/ppermute | solution.py:230
  54.8 31.6 %collective-permute-start.13 = (bf16[4,24,6912]{2,1,0:T(8,128)(2,1)S(1)}, bf16[4,24,6912]{2,1,0:T(8,128)(2,1)S(1)}, u32[]{:S(2)}, u32[]{:S(2)}) collective-permute-start(bf16[4,24,6912]{2,1,0:T(8,128)(2,1)S(1)} %pad_maximum_fusion.refs_0_), channel_id=1, source_target_pairs={{0,1},{1,0},{2,3},{3,2},{4,5},{5,4},{6,7},{7,6},{8,9},{9,8},{10,11... | collective-permute-start | bytes 3981320 | tf_op jit(solution)/shard_map/ppermute | solution.py:230
  56.4 32.1 %collective-permute-start.14 = (bf16[4,24,6912]{2,1,0:T(8,128)(2,1)S(1)}, bf16[4,24,6912]{2,1,0:T(8,128)(2,1)}, u32[]{:S(2)}, u32[]{:S(2)}) collective-permute-start(bf16[4,24,6912]{2,1,0:T(8,128)(2,1)S(1)} %pad_maximum_fusion.refs_0_), channel_id=1, source_target_pairs={{0,4},{1,5},{2,6},{3,7},{4,0},{5,1},{6,2},{7,3},{8,12},{9,13},{10,... | collective-permute-start | bytes 3981320 | tf_op jit(solution)/shard_map/ppermute | solution.py:230
  57.9 58.3 %collective-permute-start.15 = (bf16[4,24,6912]{2,1,0:T(8,128)(2,1)S(1)}, bf16[4,24,6912]{2,1,0:T(8,128)(2,1)}, u32[]{:S(2)}, u32[]{:S(2)}) collective-permute-start(bf16[4,24,6912]{2,1,0:T(8,128)(2,1)S(1)} %pad_maximum_fusion.refs_0_), channel_id=1, source_target_pairs={{0,5},{1,4},{2,7},{3,6},{4,1},{5,0},{6,3},{7,2},{8,13},{9,12},{10,... | collective-permute-start | bytes 3981320 | tf_op jit(solution)/shard_map/ppermute | solution.py:230
  58.4 102.2 %collective-permute-start.16 = (bf16[4,24,6912]{2,1,0:T(8,128)(2,1)S(1)}, bf16[4,24,6912]{2,1,0:T(8,128)(2,1)}, u32[]{:S(2)}, u32[]{:S(2)}) collective-permute-start(bf16[4,24,6912]{2,1,0:T(8,128)(2,1)S(1)} %pad_maximum_fusion.refs_0_), channel_id=1, source_target_pairs={{0,2},{1,3},{2,0},{3,1},{4,6},{5,7},{6,4},{7,5},{8,10},{9,11},{10,... | collective-permute-start | bytes 3981320 | tf_op jit(solution)/shard_map/ppermute | solution.py:230
  86.4 74.2 %collective-permute-start.17 = (bf16[4,24,6912]{2,1,0:T(8,128)(2,1)S(1)}, bf16[4,24,6912]{2,1,0:T(8,128)(2,1)S(1)}, u32[]{:S(2)}, u32[]{:S(2)}) collective-permute-start(bf16[4,24,6912]{2,1,0:T(8,128)(2,1)S(1)} %collective-permute-done.13.refs_1_), channel_id=1, source_target_pairs={{0,2},{1,3},{2,0},{3,1},{4,6},{5,7},{6,4},{7,5},{8,10},{9,11},{10,... | collective-permute-start | bytes 3981320 | tf_op jit(solution)/shard_map/ppermute | solution.py:230
  88.5 72.2 %collective-permute-start.18 = (bf16[4,24,6912]{2,1,0:T(8,128)(2,1)}, bf16[4,24,6912]{2,1,0:T(8,128)(2,1)S(1)}, u32[]{:S(2)}, u32[]{:S(2)}) collective-permute-start(bf16[4,24,6912]{2,1,0:T(8,128)(2,1)} %collective-permute-done.14.refs_2_), channel_id=1, source_target_pairs={{0,2},{1,3},{2,0},{3,1},{4,6},{5,7},{6,4},{7,5},{8,10},{9,11},{10,... | collective-permute-start | bytes 3981320 | tf_op jit(solution)/shard_map/ppermute | solution.py:230
  116.2 44.5 %collective-permute-start.19 = (bf16[4,24,6912]{2,1,0:T(8,128)(2,1)}, bf16[4,24,6912]{2,1,0:T(8,128)(2,1)S(1)}, u32[]{:S(2)}, u32[]{:S(2)}) collective-permute-start(bf16[4,24,6912]{2,1,0:T(8,128)(2,1)} %collective-permute-done.15.refs_3_), channel_id=1, source_target_pairs={{0,2},{1,3},{2,0},{3,1},{4,6},{5,7},{6,4},{7,5},{8,10},{9,11},{10,... | collective-permute-start | bytes 3981320 | tf_op jit(solution)/shard_map/ppermute | solution.py:230
  279.6 143.7 %collective-permute-start.30 = (bf16[4,2,2,24,3072]{4,3,0,2,1:T(8,128)(2,1)}, bf16[4,2,2,24,3072]{4,3,0,2,1:T(8,128)(2,1)}, u32[]{:S(2)}, u32[]{:S(2)}) collective-permute-start(bf16[4,2,2,24,3072]{4,3,0,2,1:T(8,128)(2,1)} %copy_bitcast_fusion), channel_id=1, source_target_pairs={{0,2},{1,3},{2,0},{3,1},{4,6},{5,7},{6,4},{7,5},{8,10},{9,11},{10,... | collective-permute-start | bytes 7077896 | tf_op jit(solution)/shard_map/ppermute | solution.py:230
  295.0 131.0 %collective-permute-start.29 = (bf16[4,2,2,96,768]{4,3,0,2,1:T(8,128)(2,1)}, bf16[4,2,2,96,768]{4,3,0,2,1:T(8,128)(2,1)}, u32[]{:S(2)}, u32[]{:S(2)}) collective-permute-start(bf16[4,2,2,96,768]{4,3,0,2,1:T(8,128)(2,1)} %copy_bitcast_fusion.1), channel_id=1, source_target_pairs={{0,2},{1,3},{2,0},{3,1},{4,6},{5,7},{6,4},{7,5},{8,10},{9,11},{10,... | collective-permute-start | bytes 7077896 | tf_op jit(solution)/shard_map/ppermute | solution.py:230
  296.5 120.4 %collective-permute-start.28 = (bf16[4,2,2,24,768]{4,3,0,2,1:T(8,128)(2,1)}, bf16[4,2,2,24,768]{4,3,0,2,1:T(8,128)(2,1)}, u32[]{:S(2)}, u32[]{:S(2)}) collective-permute-start(bf16[4,2,2,24,768]{4,3,0,2,1:T(8,128)(2,1)} %copy_bitcast_fusion.3), channel_id=1, source_target_pairs={{0,2},{1,3},{2,0},{3,1},{4,6},{5,7},{6,4},{7,5},{8,10},{9,11},{10,... | collective-permute-start | bytes 1769480 | tf_op jit(solution)/shard_map/ppermute | solution.py:230
  386.8 30.0 %collective-permute-start.21 = (bf16[4,2,2,24,128]{4,3,0,2,1:T(8,128)(2,1)S(1)}, bf16[4,2,2,24,128]{4,3,0,2,1:T(8,128)(2,1)S(1)}, u32[]{:S(2)}, u32[]{:S(2)}) collective-permute-start(bf16[4,2,2,24,128]{4,3,0,2,1:T(8,128)(2,1)S(1)} %copy_bitcast_fusion.4), channel_id=1, source_target_pairs={{0,2},{1,3},{2,0},{3,1},{4,6},{5,7},{6,4},{7,5},{8,10},{9,11},{10,... | collective-permute-start | bytes 294920 | tf_op jit(solution)/shard_map/ppermute | solution.py:230
  399.6 19.4 %collective-permute-start.20 = (bf16[4,2,2,24,2304]{4,3,0,2,1:T(8,128)(2,1)S(1)}, bf16[4,2,2,24,2304]{4,3,0,2,1:T(8,128)(2,1)S(1)}, u32[]{:S(2)}, u32[]{:S(2)}) collective-permute-start(bf16[4,2,2,24,2304]{4,3,0,2,1:T(8,128)(2,1)S(1)} %copy_bitcast_fusion.2), channel_id=1, source_target_pairs={{0,2},{1,3},{2,0},{3,1},{4,6},{5,7},{6,4},{7,5},{8,10},{9,11},{10,... | collective-permute-start | bytes 5308424 | tf_op jit(solution)/shard_map/ppermute | solution.py:230
  419.6 16.1 %collective-permute-start.22 = (bf16[4,24,2432]{2,1,0:T(8,128)(2,1)S(1)}, bf16[4,24,2432]{2,1,0:T(8,128)(2,1)S(1)}, u32[]{:S(2)}, u32[]{:S(2)}) collective-permute-start(bf16[4,24,2432]{2,1,0:T(8,128)(2,1)S(1)} %pad_maximum_fusion.2), channel_id=1, source_target_pairs={{0,1},{1,0},{2,3},{3,2},{4,5},{5,4},{6,7},{7,6},{8,9},{9,8},{10,11... | collective-permute-start | bytes 1400840 | tf_op jit(solution)/shard_map/ppermute | solution.py:230
  421.2 18.4 %collective-permute-start.23 = (bf16[4,24,2432]{2,1,0:T(8,128)(2,1)S(1)}, bf16[4,24,2432]{2,1,0:T(8,128)(2,1)S(1)}, u32[]{:S(2)}, u32[]{:S(2)}) collective-permute-start(bf16[4,24,2432]{2,1,0:T(8,128)(2,1)S(1)} %pad_maximum_fusion.3), channel_id=1, source_target_pairs={{0,4},{1,5},{2,6},{3,7},{4,0},{5,1},{6,2},{7,3},{8,12},{9,13},{10,... | collective-permute-start | bytes 1400840 | tf_op jit(solution)/shard_map/ppermute | solution.py:230
  422.8 22.1 %collective-permute-start.24 = (bf16[4,24,2432]{2,1,0:T(8,128)(2,1)S(1)}, bf16[4,24,2432]{2,1,0:T(8,128)(2,1)S(1)}, u32[]{:S(2)}, u32[]{:S(2)}) collective-permute-start(bf16[4,24,2432]{2,1,0:T(8,128)(2,1)S(1)} %pad_maximum_fusion.4), channel_id=1, source_target_pairs={{0,5},{1,4},{2,7},{3,6},{4,1},{5,0},{6,3},{7,2},{8,13},{9,12},{10,... | collective-permute-start | bytes 1400840 | tf_op jit(solution)/shard_map/ppermute | solution.py:230
  432.4 40.4 %collective-permute-start.31 = (bf16[4,216,768]{2,1,0:T(8,128)(2,1)}, bf16[4,216,768]{2,1,0:T(8,128)(2,1)S(1)}, u32[]{:S(2)}, u32[]{:S(2)}) collective-permute-start(bf16[4,216,768]{2,1,0:T(8,128)(2,1)} %slice_dynamic-update-slice_fusion.8), channel_id=1, source_target_pairs={{0,1},{1,0},{2,3},{3,2},{4,5},{5,4},{6,7},{7,6},{8,9},{9,8},{10,11... | collective-permute-start | bytes 3981320 | tf_op jit(solution)/shard_map/ppermute | solution.py:230
  434.0 40.0 %collective-permute-start.32 = (bf16[4,216,768]{2,1,0:T(8,128)(2,1)S(1)}, bf16[4,216,768]{2,1,0:T(8,128)(2,1)S(1)}, u32[]{:S(2)}, u32[]{:S(2)}) collective-permute-start(bf16[4,216,768]{2,1,0:T(8,128)(2,1)S(1)} %slice_dynamic-update-slice_fusion.4), channel_id=1, source_target_pairs={{0,4},{1,5},{2,6},{3,7},{4,0},{5,1},{6,2},{7,3},{8,12},{9,13},{10,... | collective-permute-start | bytes 3981320 | tf_op jit(solution)/shard_map/ppermute | solution.py:230
  435.7 64.8 %collective-permute-start.33 = (bf16[4,216,768]{2,1,0:T(8,128)(2,1)S(1)}, bf16[4,216,768]{2,1,0:T(8,128)(2,1)S(1)}, u32[]{:S(2)}, u32[]{:S(2)}) collective-permute-start(bf16[4,216,768]{2,1,0:T(8,128)(2,1)S(1)} %slice_dynamic-update-slice_fusion), channel_id=1, source_target_pairs={{0,5},{1,4},{2,7},{3,6},{4,1},{5,0},{6,3},{7,2},{8,13},{9,12},{10,... | collective-permute-start | bytes 3981320 | tf_op jit(solution)/shard_map/ppermute | solution.py:230
  445.1 58.0 %collective-permute-start.25 = (bf16[24,2432]{1,0:T(8,128)(2,1)S(1)}, bf16[24,2432]{1,0:T(8,128)(2,1)S(1)}, u32[]{:S(2)}, u32[]{:S(2)}) collective-permute-start(bf16[24,2432]{1,0:T(8,128)(2,1)S(1)} %get-tuple-element.75), channel_id=1, source_target_pairs={{0,8},{1,9},{2,10},{3,11},{4,12},{5,13},{6,14},{7,15},{8,0},{9,1},... | collective-permute-start | bytes 350216 | tf_op jit(solution)/shard_map/ppermute | solution.py:230
  446.5 59.0 %collective-permute-start.26 = (bf16[24,2432]{1,0:T(8,128)(2,1)S(1)}, bf16[24,2432]{1,0:T(8,128)(2,1)S(1)}, u32[]{:S(2)}, u32[]{:S(2)}) collective-permute-start(bf16[24,2432]{1,0:T(8,128)(2,1)S(1)} %get-tuple-element.76), channel_id=1, source_target_pairs={{0,16},{1,17},{2,18},{3,19},{4,20},{5,21},{6,22},{7,23},{8,24},{9,... | collective-permute-start | bytes 350216 | tf_op jit(solution)/shard_map/ppermute | solution.py:230
  472.8 32.7 %collective-permute-start.27 = (bf16[24,2432]{1,0:T(8,128)(2,1)S(1)}, bf16[24,2432]{1,0:T(8,128)(2,1)S(1)}, u32[]{:S(2)}, u32[]{:S(2)}) collective-permute-start(bf16[24,2432]{1,0:T(8,128)(2,1)S(1)} %get-tuple-element.77), channel_id=1, source_target_pairs={{0,24},{1,25},{2,26},{3,27},{4,28},{5,29},{6,30},{7,31},{8,16},{9,... | collective-permute-start | bytes 350216 | tf_op jit(solution)/shard_map/ppermute | solution.py:230
  501.0 14.2 %collective-permute-start.34 = (bf16[216,768]{1,0:T(8,128)(2,1)S(1)}, bf16[216,768]{1,0:T(8,128)(2,1)S(1)}, u32[]{:S(2)}, u32[]{:S(2)}) collective-permute-start(bf16[216,768]{1,0:T(8,128)(2,1)S(1)} %get-tuple-element.67), channel_id=1, source_target_pairs={{0,8},{1,9},{2,10},{3,11},{4,12},{5,13},{6,14},{7,15},{8,0},{9,1},... | collective-permute-start | bytes 995336 | tf_op jit(solution)/shard_map/ppermute | solution.py:230
  502.5 25.9 %collective-permute-start.35 = (bf16[216,768]{1,0:T(8,128)(2,1)S(1)}, bf16[216,768]{1,0:T(8,128)(2,1)S(1)}, u32[]{:S(2)}, u32[]{:S(2)}) collective-permute-start(bf16[216,768]{1,0:T(8,128)(2,1)S(1)} %get-tuple-element.69), channel_id=1, source_target_pairs={{0,16},{1,17},{2,18},{3,19},{4,20},{5,21},{6,22},{7,23},{8,24},{9,... | collective-permute-start | bytes 995336 | tf_op jit(solution)/shard_map/ppermute | solution.py:230
  503.1 25.2 %collective-permute-start.36 = (bf16[216,768]{1,0:T(8,128)(2,1)S(1)}, bf16[216,768]{1,0:T(8,128)(2,1)S(1)}, u32[]{:S(2)}, u32[]{:S(2)}) collective-permute-start(bf16[216,768]{1,0:T(8,128)(2,1)S(1)} %get-tuple-element.68), channel_id=1, source_target_pairs={{0,24},{1,25},{2,26},{3,27},{4,28},{5,29},{6,30},{7,31},{8,16},{9,... | collective-permute-start | bytes 995336 | tf_op jit(solution)/shard_map/ppermute | solution.py:230
  (49 other events, 721.1 us)
